TPU v7x, 32 devices: a whole 2x2x4 slice. The times are simulated.
32 devices in a mesh: row: 8 (over y, x, core), cent: 4 (over z).
Axes of the slice: x: 2, y: 2, z: 4, core: 2. Of those that a mesh axis runs over, the one named last changes fastest.
Arguments:
- embeddings: bfloat16 [4096, 1536], P('row'), may hold values from -48 to 48
- centroids: bfloat16 [1024, 1536], P('cent'), may hold values from -0.5 to 0.5
Outputs:
- centroids_out: bfloat16 [1024, 1536], P('cent')
- energy: float32 [4096], P('row')
All inputs are finite; a program needn't handle non-finite values.
Results may differ from a plain program's by a relative error of at most 0.0091.
Values may be sent and summed in bfloat16 or wider, within the bound.
A program may use at most 64 MiB of HBM per device.

v0:
```python
import jax
import jax.numpy as jnp
from jax import lax
from jax.sharding import PartitionSpec as P

ITERS = 2


PRIOR_WEIGHT = 8.0


def score_against(embeddings, cluster_block):
    squared = jnp.sum(jnp.square(cluster_block.astype(jnp.float32)), axis=1)
    inner = lax.dot_general(
        embeddings, cluster_block, (((1,), (1,)), ((), ())), preferred_element_type=jnp.float32
    )
    return inner - 0.5 * squared[None, :]


def updated_rows(totals, mass, previous):
    blended = (totals + PRIOR_WEIGHT * previous.astype(jnp.float32)) / (mass + PRIOR_WEIGHT)[
        :, None
    ]
    return blended.astype(jnp.bfloat16)


def local(embeddings, centroids):
    row_count = embeddings.shape[0]
    cluster_count = centroids.shape[0]
    share_rows = cluster_count // lax.axis_size("row")
    shares = lax.dynamic_slice_in_dim(centroids, lax.axis_index("row") * share_rows, share_rows, 0)
    energy = jnp.zeros((row_count,), jnp.float32)
    for iteration in range(ITERS):
        if iteration == 0:
            scores = score_against(embeddings, centroids)
        else:
            scores = score_against(embeddings, lax.all_gather(shares, "row", axis=0, tiled=True))
        row_top = lax.pmax(jnp.max(scores, axis=1), "cent")
        lifted = jnp.exp(scores - row_top[:, None])
        row_total = lax.psum(jnp.sum(lifted, axis=1), "cent")
        weights = (lifted / row_total[:, None]).astype(jnp.bfloat16)
        totals = lax.dot_general(
            weights, embeddings, (((0,), (0,)), ((), ())), preferred_element_type=jnp.float32
        )
        mass = jnp.sum(weights.astype(jnp.float32), axis=0)
        energies = row_top + jnp.log(row_total)
        if iteration == 0:
            energy = energies
        share_totals, share_mass = (
            lax.psum_scatter(totals, "row", scatter_dimension=0, tiled=True),
            lax.psum_scatter(mass, "row", scatter_dimension=0, tiled=True),
        )
        shares = updated_rows(share_totals, share_mass, shares)
    result = lax.all_gather(shares, "row", axis=0, tiled=True)
    return (result, energy)


def solution(mesh):
    return jax.shard_map(
        local,
        mesh=mesh,
        in_specs=(P("row", None), P("cent", None)),
        out_specs=(P("cent", None), P("row")),
        check_vma=False,
    )
```

profile of v0, /device:TPU:1, one launch (start us, length us, event | category | flops | bytes accessed | tf_op | source)
XLA Modules:
  0.0 163.4 jit_solution(7746312967549829049)
XLA Ops:
  7.2 0.0 copy-start
  7.2 0.0 reduce-scatter.3.cloned.1.call-start
  7.2 1.5 multiply_reduce_fusion.1
  8.7 0.1 copy-done
  8.8 1.7 %fusion.2 = (f32[512]{0:T(512)S(1)}, f32[512,256]{0,1:T(8,128)S(1)}) fusion(f32[256]{0:T(256)S(1)} %broadcast_multiply_fusion.1, bf16[512,1536]{1,0:T(8,128)(2,1)S(1)} %copy-done, bf16[256,1536]{1,0:T(8,128)(2,1)} %param.3), kind=kOutput, calls=%fused_computation.19 | convolution fusion | flops 402914816 | bytes 2886656 | tf_op jit(solution)/shard_map/dot_general | solution.py:14
  10.6 10.8 %pmax.14 = f32[512]{0:T(512)S(1)} all-reduce(f32[512]{0:T(512)S(1)} %get-tuple-element.6), channel_id=1, replica_groups=mesh['row'=8,'cent'=4] {'cent'}, use_global_device_ids=true, to_apply=%region_2.0 | all-reduce | flops 512 | bytes 4096 | tf_op jit(solution)/shard_map/pmax | solution.py:38
  21.3 0.1 fusion
  21.5 6.6 %psum.14 = f32[512]{0:T(512)S(1)} all-reduce(f32[512]{0:T(512)S(1)} %fusion), channel_id=1, replica_groups=mesh['row'=8,'cent'=4] {'cent'}, use_global_device_ids=true, to_apply=%region_4.0 | all-reduce | flops 512 | bytes 4096 | tf_op jit(solution)/shard_map/psum | solution.py:40
  28.1 0.2 convert_reduce_fusion.1
  28.3 1.7 %fusion.4 = f32[256,1536]{1,0:T(8,128)} fusion(bf16[512,256]{0,1:T(8,128)(2,1)S(1)} %get-tuple-element.5, bf16[512,1536]{1,0:T(8,128)(2,1)S(1)} %copy-done), kind=kOutput, calls=%fused_computation.21 | convolution fusion | flops 402653184 | bytes 3407872 | tf_op jit(solution)/shard_map/dot_general | solution.py:42
  30.0 0.0 copy-start.1
  30.0 0.0 reduce-scatter.3.cloned.1.call-update
  30.0 0.0 reduce-scatter.5.cloned.1.call-start
  30.1 0.6 copy-done.1
  30.6 0.6 dynamic-slice
  31.9 15.6 %all-reduce = f32[256]{0:T(256)S(1)} all-reduce(f32[256]{0:T(256)S(1)} %get-tuple-element.4), channel_id=3, replica_groups=mesh['row'=8,'cent'=4] {'row'}, use_global_device_ids=true, to_apply=%region_7.0.clone | all-reduce | flops 256 | bytes 2048
  47.5 0.1 dynamic-slice_add_fusion.1
  47.6 24.5 %reduce-scatter.3.cloned.1.call-done = f32[32,1536]{1,0:T(8,128)} async-done(((f32[256,1536]{1,0:T(8,128)}), f32[32,1536]{1,0:T(8,128)}) %reduce-scatter.3.cloned.1.call-update) | async-done | bytes 196624 | tf_op jit(solution)/shard_map/reduce_scatter | solution.py:50
  72.1 1.1 divide_convert_fusion.3
  73.2 10.9 %all_gather.6 = bf16[256,1536]{1,0:T(8,128)(2,1)S(1)} all-gather(bf16[32,1536]{1,0:T(8,128)(2,1)S(1)} %divide_convert_fusion.3), channel_id=1, replica_groups=mesh['row'=8,'cent'=4] {'row'}, dimensions={0}, use_global_device_ids=true | all-gather | bytes 884736 | tf_op jit(solution)/shard_map/all_gather | solution.py:37
  84.0 0.2 multiply_reduce_fusion
  84.3 0.6 fusion.3
  84.9 9.7 %pmax.15 = f32[512]{0:T(512)S(1)} all-reduce(f32[512]{0:T(512)S(1)} %get-tuple-element.8), channel_id=1, replica_groups=mesh['row'=8,'cent'=4] {'cent'}, use_global_device_ids=true, to_apply=%region_10.0 | all-reduce | flops 512 | bytes 4096 | tf_op jit(solution)/shard_map/pmax | solution.py:38
  94.6 0.1 fusion.1
  94.7 6.6 %psum.15 = f32[512]{0:T(512)S(1)} all-reduce(f32[512]{0:T(512)S(1)} %fusion.1), channel_id=1, replica_groups=mesh['row'=8,'cent'=4] {'cent'}, use_global_device_ids=true, to_apply=%region_12.0 | all-reduce | flops 512 | bytes 4096 | tf_op jit(solution)/shard_map/psum | solution.py:40
  101.3 0.2 convert_reduce_fusion
  101.5 1.7 %fusion.5 = f32[256,1536]{1,0:T(8,128)} fusion(bf16[256,512]{1,0:T(8,128)(2,1)S(1)} %get-tuple-element.3, bf16[512,1536]{1,0:T(8,128)(2,1)S(1)} %copy-done), kind=kOutput, calls=%fused_computation.22 | convolution fusion | flops 402653184 | bytes 3407872 | tf_op jit(solution)/shard_map/dot_general | solution.py:42
  103.2 0.0 reduce-scatter.5.cloned.1.call-update
  103.2 0.6 log_add_fusion
  103.8 15.0 %all-reduce.1 = f32[256]{0:T(256)S(1)} all-reduce(f32[256]{0:T(256)S(1)} %get-tuple-element.2), channel_id=5, replica_groups=mesh['row'=8,'cent'=4] {'row'}, use_global_device_ids=true, to_apply=%region_15.0.clone | all-reduce | flops 256 | bytes 2048
  118.9 0.1 dynamic-slice_add_fusion
  119.0 24.8 %reduce-scatter.5.cloned.1.call-done = f32[32,1536]{1,0:T(8,128)} async-done(((f32[256,1536]{1,0:T(8,128)}), f32[32,1536]{1,0:T(8,128)}) %reduce-scatter.5.cloned.1.call-update) | async-done | bytes 196624 | tf_op jit(solution)/shard_map/reduce_scatter | solution.py:50
  143.8 1.0 divide_convert_fusion.2
  144.8 10.9 %all_gather.7 = bf16[256,1536]{1,0:T(8,128)(2,1)S(1)} all-gather(bf16[32,1536]{1,0:T(8,128)(2,1)S(1)} %divide_convert_fusion.2), channel_id=1, replica_groups=mesh['row'=8,'cent'=4] {'row'}, dimensions={0}, use_global_device_ids=true | all-gather | bytes 884736 | tf_op jit(solution)/shard_map/all_gather | solution.py:54
  155.7 0.9 copy.5
  (2 shorter events, 0.0 us)
Async XLA Ops:
  7.2 1.7 %copy-start = (bf16[512,1536]{1,0:T(8,128)(2,1)S(1)}, bf16[512,1536]{1,0:T(8,128)(2,1)}, u32[]{:S(2)}) copy-start(bf16[512,1536]{1,0:T(8,128)(2,1)} %param.2) | copy-start | bytes 4718596
  7.2 64.9 %reduce-scatter.3.cloned.1.call-start = ((), (), s32[]{:S(2)}) async-start(), calls=%async_computation.2 | async-start | bytes 1769472 | tf_op jit(solution)/shard_map/reduce_scatter | solution.py:50
  30.0 0.7 copy-start.1
  30.0 113.7 %reduce-scatter.5.cloned.1.call-start = ((), (), s32[]{:S(2)}) async-start(), calls=%async_computation.3 | async-start | bytes 1769472 | tf_op jit(solution)/shard_map/reduce_scatter | solution.py:50
Sparse Core Ops, SparseCore 0:
  30.1 41.8 reduce-scatter.2
  103.4 40.3 reduce-scatter.4
where the time goes:
time: 164 us; the launch traced here: 163 us
  blocking collectives  86.1 us (52%)
  waiting for transfers between devices  49.3 us (30%)
  between operations  14.7 us (9%)
  matrix products  5.83 us (4%)
  other arithmetic  5.14 us (3%)
  local copies, waits for them, and re-layouts  2.15 us (1%)
    reduce_scatter x2, waiting for transfers between devices, local(): lax.psum_scatter(totals, 'row', scatter_dimension=0, tiled=True)  49.3 us
    unnamed x2, blocking collectives  30.7 us
    pmax x2, blocking collectives, local(): row_top = lax.pmax(jnp.max(scores, axis=1), 'cent')  20.5 us
    psum x2, blocking collectives, local(): row_total = lax.psum(jnp.sum(lifted, axis=1), 'cent')  13.2 us
    all_gather x1, blocking collectives, local(): result = lax.all_gather(shares, 'row', axis=0, tiled=True)  10.9 us
    all_gather x1, blocking collectives, local(): lax.all_gather(shares, 'row', axis=0, tiled=True)  10.9 us
    dot_general x2, matrix products, local(): lax.dot_general(weights, embeddings, (((0,), (0,)), ((), ())), preferred_...  3.46 us
  transfers between devices with their start and end apart: 2, of which 2 were waited for; matrix products, arithmetic and copies ran while one was open for 1% of the time, Pallas kernels for 0%

commit v1 on v0

--- a/solution.py
+++ b/solution.py
@@ -1,19 +1,22 @@
+import functools
+
 import jax
 import jax.numpy as jnp
 from jax import lax
+from jax.experimental import pallas as pl
+from jax.experimental.pallas import tpu as pltpu
 from jax.sharding import PartitionSpec as P
 
 ITERS = 2
-
-
 PRIOR_WEIGHT = 8.0
+CHUNKS = 2
+MESH = pl.DeviceIdType.MESH
+NT = (((1,), (1,)), ((), ()))
 
 
 def score_against(embeddings, cluster_block):
     squared = jnp.sum(jnp.square(cluster_block.astype(jnp.float32)), axis=1)
-    inner = lax.dot_general(
-        embeddings, cluster_block, (((1,), (1,)), ((), ())), preferred_element_type=jnp.float32
-    )
+    inner = lax.dot_general(embeddings, cluster_block, NT, preferred_element_type=jnp.float32)
     return inner - 0.5 * squared[None, :]
 
 
@@ -24,7 +27,7 @@
     return blended.astype(jnp.bfloat16)
 
 
-def local(embeddings, centroids):
+def local_plain(embeddings, centroids):
     row_count = embeddings.shape[0]
     cluster_count = centroids.shape[0]
     share_rows = cluster_count // lax.axis_size("row")
@@ -55,7 +58,300 @@
     return (result, energy)
 
 
+def kernel(
+    groups, chunks,
+    x_hbm, c_hbm, out_hbm, energy_ref,
+    xs, cs, wt, st, sq, mass_col,
+    stat_send, stat_recv, mass_send, mass_recv,
+    s0, r0, k0, s1, r1, k1, s2, r2, k2, cc,
+    load_sem, out_sem, stat_ss, stat_rs, mass_ss, mass_rs, ring_ss, ring_rs,
+):
+    rows, depth = xs.shape
+    count = cs.shape[0]
+    width = depth // chunks
+    half, quarter, eighth = count // 2, count // 4, count // 8
+    r = lax.axis_index("row")
+    z = lax.axis_index("cent")
+    core = lax.rem(r, 2)
+    px = lax.rem(r // 2, 2)
+    py = r // 4
+    sibling = r + 1 - 2 * core
+    flip_x = 2 * (1 - 2 * px)
+    flip_y = 4 * (1 - 2 * py)
+    first = r + (1 - core) * flip_x + core * flip_y
+    second = r + core * flip_x + (1 - core) * flip_y
+    a = (1 - core) * px + core * py
+    b = (1 - core) * py + core * px
+    base_half = pl.multiple_of(core * half, half)
+    other_half = pl.multiple_of((1 - core) * half, half)
+    base_quarter = pl.multiple_of(core * half + a * quarter, quarter)
+    base = pl.multiple_of(core * half + a * quarter + b * eighth, eighth)
+    mine_q = pl.multiple_of(a * quarter, quarter)
+    theirs_q = pl.multiple_of((1 - a) * quarter, quarter)
+    mine_e = pl.multiple_of(b * eighth, eighth)
+    theirs_e = pl.multiple_of((1 - b) * eighth, eighth)
+
+    barrier = pltpu.get_barrier_semaphore()
+    for d in range(1, 8):
+        pl.semaphore_signal(
+            barrier, inc=1, device_id=(lax.rem(r + d, 8), z), device_id_type=MESH
+        )
+    for d in range(1, groups):
+        pl.semaphore_signal(
+            barrier, inc=1, device_id=(r, lax.rem(z + d, groups)), device_id_type=MESH
+        )
+    loads = [
+        pltpu.make_async_copy(c_hbm, cs, load_sem.at[0]),
+        pltpu.make_async_copy(x_hbm, xs, load_sem.at[1]),
+    ]
+    for load in loads:
+        load.start()
+
+    sends = []
+
+    def remote(src, dst, ss, rs, device):
+        copy = pltpu.make_async_remote_copy(
+            src_ref=src, dst_ref=dst, send_sem=ss, recv_sem=rs,
+            device_id=device, device_id_type=MESH,
+        )
+        copy.start()
+        sends.append(copy)
+        return copy
+
+    def cols(j):
+        return pl.ds(j * width, width)
+
+    def norms(block):
+        wide = block.astype(jnp.float32)
+        return jnp.sum(wide * wide, axis=1, keepdims=True)
+
+    for load in loads:
+        load.wait()
+    st[...] = lax.dot_general(cs[...], xs[...], NT, preferred_element_type=jnp.float32)
+    sq[...] = norms(cs[...])
+
+    for it in range(ITERS):
+        shifted = st[...] - 0.5 * sq[...]
+        top = jnp.max(shifted, axis=0, keepdims=True)
+        lifted = jnp.exp(shifted - top)
+        total = jnp.sum(lifted, axis=0, keepdims=True)
+        stat_send[it, 0:1, :] = top
+        stat_send[it, 1:2, :] = total
+        if it == 0:
+            pl.semaphore_wait(barrier, 7 + groups - 1)
+        arrivals = []
+        for d in range(1, groups):
+            arrivals.append(
+                remote(
+                    stat_send.at[it], stat_recv.at[it, d - 1],
+                    stat_ss.at[it, d - 1], stat_rs.at[it, d - 1],
+                    (r, lax.rem(z + d, groups)),
+                )
+            )
+        st[...] = lifted
+        all_top, tops, sums = top, [top], [total]
+        for d in range(1, groups):
+            arrivals[d - 1].wait_recv()
+            tops.append(stat_recv[it, d - 1, 0:1, :])
+            sums.append(stat_recv[it, d - 1, 1:2, :])
+            all_top = jnp.maximum(all_top, tops[-1])
+        all_total = jnp.zeros_like(total)
+        for t, s in zip(tops, sums):
+            all_total = all_total + s * jnp.exp(t - all_top)
+        if it == 0:
+            energy_ref[...] = all_top + jnp.log(all_total)
+        scale = jnp.exp(top - all_top) / all_total
+        weights = (st[...] * scale).astype(jnp.bfloat16)
+        wt[...] = weights
+
+        mass_send[it] = lax.dot_general(
+            jnp.ones((8, rows), jnp.bfloat16), weights, NT, preferred_element_type=jnp.float32
+        )
+        masses = []
+
+        def send_masses(it=it, masses=masses):
+            for d in range(1, 8):
+                masses.append(
+                    remote(
+                        mass_send.at[it], mass_recv.at[it, d - 1],
+                        mass_ss.at[it, d - 1], mass_rs.at[it, d - 1],
+                        (lax.rem(r + d, 8), z),
+                    )
+                )
+
+        flights = {}
+
+        def stage0(j, it=it):
+            part = jnp.dot(
+                wt[pl.ds(other_half, half), :], xs[:, cols(j)], preferred_element_type=jnp.float32
+            )
+            s0[it, j] = part.astype(jnp.bfloat16)
+            flights[0, j] = remote(
+                s0.at[it, j], r0.at[it, j], ring_ss.at[it, j, 0], ring_rs.at[it, j, 0], (sibling, z)
+            )
+            if j == 0:
+                send_masses()
+            k0[j] = jnp.dot(
+                wt[pl.ds(base_half, half), :], xs[:, cols(j)], preferred_element_type=jnp.float32
+            )
+
+        def stage1(j, it=it):
+            flights[0, j].wait_recv()
+            there, here = pl.ds(theirs_q, quarter), pl.ds(mine_q, quarter)
+            s1[it, j] = (k0[j, there] + r0[it, j, there].astype(jnp.float32)).astype(jnp.bfloat16)
+            flights[1, j] = remote(
+                s1.at[it, j], r1.at[it, j], ring_ss.at[it, j, 1], ring_rs.at[it, j, 1], (first, z)
+            )
+            k1[j] = k0[j, here] + r0[it, j, here].astype(jnp.float32)
+
+        def stage2(j, it=it):
+            flights[1, j].wait_recv()
+            there, here = pl.ds(theirs_e, eighth), pl.ds(mine_e, eighth)
+            s2[it, j] = (k1[j, there] + r1[it, j, there].astype(jnp.float32)).astype(jnp.bfloat16)
+            flights[2, j] = remote(
+                s2.at[it, j], r2.at[it, j], ring_ss.at[it, j, 2], ring_rs.at[it, j, 2], (second, z)
+            )
+            k2[j] = k1[j, here] + r1[it, j, here].astype(jnp.float32)
+            if j == 0:
+                everyone = mass_send[it]
+                for d in range(1, 8):
+                    masses[d - 1].wait_recv()
+                    everyone = everyone + mass_recv[it, d - 1]
+                tall = jnp.concatenate([everyone] * 16, axis=0)
+                mass_col[...] = 1.0 / (jnp.transpose(tall) + PRIOR_WEIGHT)
+
+        def stage3(j, it=it):
+            flights[2, j].wait_recv()
+            mine = pl.ds(base, eighth)
+            old = cs[mine, cols(j)] if it == 0 else cc[it - 1, j, mine]
+            sums = k2[j] + r2[it, j].astype(jnp.float32) + PRIOR_WEIGHT * old.astype(jnp.float32)
+            cc[it, j, mine] = (sums * mass_col[mine, 0:1]).astype(jnp.bfloat16)
+            place = cc.at[it, j, mine]
+            flights[3, j] = remote(
+                place, place, ring_ss.at[it, j, 3], ring_rs.at[it, j, 3], (second, z)
+            )
+
+        def stage4(j, it=it):
+            flights[3, j].wait_recv()
+            place = cc.at[it, j, pl.ds(base_quarter, quarter)]
+            flights[4, j] = remote(
+                place, place, ring_ss.at[it, j, 4], ring_rs.at[it, j, 4], (first, z)
+            )
+
+        def stage5(j, it=it):
+            flights[4, j].wait_recv()
+            place = cc.at[it, j, pl.ds(base_half, half)]
+            flights[5, j] = remote(
+                place, place, ring_ss.at[it, j, 5], ring_rs.at[it, j, 5], (sibling, z)
+            )
+
+        def stage6(j, it=it):
+            flights[5, j].wait_recv()
+            if it == ITERS - 1:
+                copy = pltpu.make_async_copy(cc.at[it, j], out_hbm.at[:, cols(j)], out_sem.at[j])
+                copy.start()
+                outs.append(copy)
+                return
+            block = cc[it, j]
+            inner = lax.dot_general(block, xs[:, cols(j)], NT, preferred_element_type=jnp.float32)
+            if j == 0:
+                st[...] = inner
+                sq[...] = norms(block)
+            else:
+                st[...] += inner
+                sq[...] += norms(block)
+
+        outs = []
+        stages = [stage0, stage1, stage2, stage3, stage4, stage5, stage6]
+        for tick in range(chunks + len(stages) - 1):
+            for s in reversed(range(len(stages))):
+                if 0 <= tick - s < chunks:
+                    stages[s](tick - s)
+        for copy in outs:
+            copy.wait()
+
+    for copy in sends:
+        copy.wait_send()
+
+
+def local_fused(groups, embeddings, centroids):
+    rows, depth = embeddings.shape
+    count = centroids.shape[0]
+    chunks = CHUNKS
+    width = depth // chunks
+    half, quarter, eighth = count // 2, count // 4, count // 8
+    bf16, f32 = jnp.bfloat16, jnp.float32
+    dma = pltpu.SemaphoreType.DMA
+    result, energy = pl.pallas_call(
+        functools.partial(kernel, groups, chunks),
+        out_shape=(
+            jax.ShapeDtypeStruct((count, depth), bf16),
+            jax.ShapeDtypeStruct((1, rows), f32),
+        ),
+        in_specs=[pl.BlockSpec(memory_space=pl.ANY)] * 2,
+        out_specs=(
+            pl.BlockSpec(memory_space=pl.ANY),
+            pl.BlockSpec(memory_space=pltpu.VMEM),
+        ),
+        scratch_shapes=[
+            pltpu.VMEM((rows, depth), bf16),
+            pltpu.VMEM((count, depth), bf16),
+            pltpu.VMEM((count, rows), bf16),
+            pltpu.VMEM((count, rows), f32),
+            pltpu.VMEM((count, 1), f32),
+            pltpu.VMEM((count, 128), f32),
+            pltpu.VMEM((ITERS, 2, rows), f32),
+            pltpu.VMEM((ITERS, groups - 1, 2, rows), f32),
+            pltpu.VMEM((ITERS, 8, count), f32),
+            pltpu.VMEM((ITERS, 7, 8, count), f32),
+            pltpu.VMEM((ITERS, chunks, half, width), bf16),
+            pltpu.VMEM((ITERS, chunks, half, width), bf16),
+            pltpu.VMEM((chunks, half, width), f32),
+            pltpu.VMEM((ITERS, chunks, quarter, width), bf16),
+            pltpu.VMEM((ITERS, chunks, quarter, width), bf16),
+            pltpu.VMEM((chunks, quarter, width), f32),
+            pltpu.VMEM((ITERS, chunks, eighth, width), bf16),
+            pltpu.VMEM((ITERS, chunks, eighth, width), bf16),
+            pltpu.VMEM((chunks, eighth, width), f32),
+            pltpu.VMEM((ITERS, chunks, count, width), bf16),
+            dma((2,)),
+            dma((chunks,)),
+            dma((ITERS, groups - 1)),
+            dma((ITERS, groups - 1)),
+            dma((ITERS, 7)),
+            dma((ITERS, 7)),
+            dma((ITERS, chunks, 6)),
+            dma((ITERS, chunks, 6)),
+        ],
+        compiler_params=pltpu.CompilerParams(
+            collective_id=0, has_side_effects=True, vmem_limit_bytes=48 * 1024 * 1024
+        ),
+        cost_estimate=pl.CostEstimate(
+            flops=8 * rows * count * depth,
+            bytes_accessed=2 * depth * (rows + 2 * count),
+            transcendentals=2 * rows * count,
+        ),
+    )(embeddings, centroids)
+    return result, energy.reshape(rows)
+
+
 def solution(mesh):
+    def local(embeddings, centroids):
+        rows, depth = embeddings.shape
+        count = centroids.shape[0]
+        groups = mesh.shape["cent"]
+        fits = (
+            mesh.shape["row"] == 8
+            and groups > 1
+            and rows % 256 == 0
+            and rows <= 1024
+            and count == 256
+            and depth % (128 * CHUNKS) == 0
+        )
+        if fits:
+            return local_fused(groups, embeddings, centroids)
+        return local_plain(embeddings, centroids)
+
     return jax.shard_map(
         local,
         mesh=mesh,

time: 164 us -> 59.5 us (0.36)
  blocking collectives: 86.1 us -> 0 us
  Pallas kernels: 0 us -> 54.7 us
  waiting for transfers between devices: 49.3 us -> 0 us
  between operations: 14.7 us -> 0.65 us
  matrix products: 5.83 us -> 0 us
  other arithmetic: 5.14 us -> 0 us
  local copies, waits for them, and re-layouts: 2.15 us -> 3.99 us
    pallas_call x0 -> x1, Pallas kernels: none -> 54.7 us  [local_fused(): pl.pallas_call(functools.partial(kernel, groups, chunks), out_shape=(jax....]
    reduce_scatter x2 -> x0, waiting for transfers between devices: 49.3 us -> none  [local(): lax.psum_scatter(totals, 'row', scatter_dimension=0, tiled=True)]
    unnamed x2 -> x0, blocking collectives: 30.7 us -> none
    all_gather x2 -> x0, blocking collectives: 21.8 us -> none  [the longest x1 10.9 us: local(): result = lax.all_gather(shares, 'row', axis=0, tiled=True)]
    pmax x2 -> x0, blocking collectives: 20.5 us -> none  [local(): row_top = lax.pmax(jnp.max(scores, axis=1), 'cent')]
    psum x2 -> x0, blocking collectives: 13.2 us -> none  [local(): row_total = lax.psum(jnp.sum(lifted, axis=1), 'cent')]
    dot_general x4 -> x0, matrix products: 5.83 us -> none  [the longest x2 3.46 us: local(): lax.dot_general(weights, embeddings, (((0,), (0,)), ((), ())), preferred_...]
    reduce_sum x6 -> x0, other arithmetic: 2.3 us -> none  [the longest x2 1.71 us: score_against(): squared = jnp.sum(jnp.square(cluster_block.astype(jnp.float32)), axis=1)]
  transfers between devices with their start and end apart: 2 -> 0, of which waited for: 2 -> 0; matrix products, arithmetic and copies ran while one was open for 1% -> 0% of each run, Pallas kernels for 0% -> 0%
where the time goes in v1:
time: 59.5 us; the launch traced here: 59.3 us
  Pallas kernels  54.7 us (92%)
  local copies, waits for them, and re-layouts  3.99 us (7%)
  between operations  0.65 us (1%)
    pallas_call x1, Pallas kernels, local_fused(): pl.pallas_call(functools.partial(kernel, groups, chunks), out_shape=(jax....  54.7 us
    unnamed x6, local copies, waits for them, and re-layouts  3.99 us

profile of v1, /device:TPU:1, one launch (start us, length us, event | category | flops | bytes accessed | tf_op | source)
XLA Modules:
  0.0 59.3 jit_solution(3244788355179609850)
XLA Ops:
  0.6 0.0 copy-start
  0.6 1.4 %copy-done = bf16[512,1536]{1,0:T(8,128)(2,1)S(1)} copy-done((bf16[512,1536]{1,0:T(8,128)(2,1)S(1)}, bf16[512,1536]{1,0:T(8,128)(2,1)}, u32[]{:S(2)}) %copy-start) | copy-done | bytes 1572888
  2.0 0.0 copy-start.1
  2.0 1.1 %copy-done.1 = bf16[256,1536]{1,0:T(8,128)(2,1)S(1)} copy-done((bf16[256,1536]{1,0:T(8,128)(2,1)S(1)}, bf16[256,1536]{1,0:T(8,128)(2,1)}, u32[]{:S(2)}) %copy-start.1) | copy-done | bytes 786456
  3.2 54.7 %shard_map.41 = (bf16[256,1536]{1,0:T(8,128)(2,1)S(1)}, f32[1,512]{1,0:T(1,128)S(1)}) custom-call(bf16[512,1536]{1,0:T(8,128)(2,1)S(1)} %copy-done, bf16[256,1536]{1,0:T(8,128)(2,1)S(1)} %copy-done.1), custom_call_target="tpu_custom_call" | custom-call | flops 1610612736 | bytes 3145728 | tf_op jit(solution)/shard_map/pallas_call | solution.py:285
  57.9 0.9 %copy.6 = bf16[256,1536]{1,0:T(8,128)(2,1)} copy(bf16[256,1536]{1,0:T(8,128)(2,1)S(1)} %get-tuple-element.8) | data formatting | bytes 1572864
  58.7 0.6 copy.7
Async XLA Ops:
  0.6 1.4 %copy-start = (bf16[512,1536]{1,0:T(8,128)(2,1)S(1)}, bf16[512,1536]{1,0:T(8,128)(2,1)}, u32[]{:S(2)}) copy-start(bf16[512,1536]{1,0:T(8,128)(2,1)} %x_hbm.1) | copy-start | bytes 4718596
  2.0 1.1 %copy-start.1 = (bf16[256,1536]{1,0:T(8,128)(2,1)S(1)}, bf16[256,1536]{1,0:T(8,128)(2,1)}, u32[]{:S(2)}) copy-start(bf16[256,1536]{1,0:T(8,128)(2,1)} %c_hbm.1) | copy-start | bytes 2359300

commit v2 on v1

--- a/solution.py
+++ b/solution.py
@@ -63,42 +63,38 @@
     x_hbm, c_hbm, out_hbm, energy_ref,
     xs, cs, wt, st, sq, mass_col,
     stat_send, stat_recv, mass_send, mass_recv,
-    s0, r0, k0, s1, r1, k1, s2, r2, k2, cc,
+    s0, r0, k0, s1, r1, cc,
     load_sem, out_sem, stat_ss, stat_rs, mass_ss, mass_rs, ring_ss, ring_rs,
 ):
     rows, depth = xs.shape
     count = cs.shape[0]
     width = depth // chunks
-    half, quarter, eighth = count // 2, count // 4, count // 8
+    half, share = count // 2, count // 8
     r = lax.axis_index("row")
     z = lax.axis_index("cent")
     core = lax.rem(r, 2)
     px = lax.rem(r // 2, 2)
     py = r // 4
     sibling = r + 1 - 2 * core
-    flip_x = 2 * (1 - 2 * px)
-    flip_y = 4 * (1 - 2 * py)
-    first = r + (1 - core) * flip_x + core * flip_y
-    second = r + core * flip_x + (1 - core) * flip_y
-    a = (1 - core) * px + core * py
-    b = (1 - core) * py + core * px
+    flips = (1 - 2 * px, 2 * (1 - 2 * py), 1 - 2 * px + 2 * (1 - 2 * py))
+    chip = r // 2
     base_half = pl.multiple_of(core * half, half)
     other_half = pl.multiple_of((1 - core) * half, half)
-    base_quarter = pl.multiple_of(core * half + a * quarter, quarter)
-    base = pl.multiple_of(core * half + a * quarter + b * eighth, eighth)
-    mine_q = pl.multiple_of(a * quarter, quarter)
-    theirs_q = pl.multiple_of((1 - a) * quarter, quarter)
-    mine_e = pl.multiple_of(b * eighth, eighth)
-    theirs_e = pl.multiple_of((1 - b) * eighth, eighth)
+
+    def part(owner):
+        return pl.ds(pl.multiple_of(owner * share, share), share)
+
+    def place(core_of, owner):
+        return pl.ds(pl.multiple_of(core_of * half + owner * share, share), share)
 
     barrier = pltpu.get_barrier_semaphore()
+    for d in range(1, groups):
+        pl.semaphore_signal(
+            barrier, inc=1, device_id=(r, lax.rem(z + d, groups)), device_id_type=MESH
+        )
     for d in range(1, 8):
         pl.semaphore_signal(
             barrier, inc=1, device_id=(lax.rem(r + d, 8), z), device_id_type=MESH
-        )
-    for d in range(1, groups):
-        pl.semaphore_signal(
-            barrier, inc=1, device_id=(r, lax.rem(z + d, groups)), device_id_type=MESH
         )
     loads = [
         pltpu.make_async_copy(c_hbm, cs, load_sem.at[0]),
@@ -161,15 +157,28 @@
         if it == 0:
             energy_ref[...] = all_top + jnp.log(all_total)
         scale = jnp.exp(top - all_top) / all_total
-        weights = (st[...] * scale).astype(jnp.bfloat16)
-        wt[...] = weights
-
-        mass_send[it] = lax.dot_general(
-            jnp.ones((8, rows), jnp.bfloat16), weights, NT, preferred_element_type=jnp.float32
-        )
+        wt[...] = (st[...] * scale).astype(jnp.bfloat16)
+
         masses = []
-
-        def send_masses(it=it, masses=masses):
+        flights = {}
+        outs = []
+
+        def sums0(j, it=it):
+            piece = jnp.dot(
+                wt[pl.ds(other_half, half), :], xs[:, cols(j)], preferred_element_type=jnp.float32
+            )
+            s0[it, j] = piece.astype(jnp.bfloat16)
+            flights[0, j] = remote(
+                s0.at[it, j], r0.at[it, j], ring_ss.at[it, j, 0], ring_rs.at[it, j, 0], (sibling, z)
+            )
+            k0[j] = jnp.dot(
+                wt[pl.ds(base_half, half), :], xs[:, cols(j)], preferred_element_type=jnp.float32
+            )
+
+        def send_masses(it=it):
+            mass_send[it] = lax.dot_general(
+                jnp.ones((8, rows), jnp.bfloat16), wt[...], NT, preferred_element_type=jnp.float32
+            )[0:1, :]
             for d in range(1, 8):
                 masses.append(
                     remote(
@@ -179,78 +188,67 @@
                     )
                 )
 
-        flights = {}
-
-        def stage0(j, it=it):
-            part = jnp.dot(
-                wt[pl.ds(other_half, half), :], xs[:, cols(j)], preferred_element_type=jnp.float32
-            )
-            s0[it, j] = part.astype(jnp.bfloat16)
-            flights[0, j] = remote(
-                s0.at[it, j], r0.at[it, j], ring_ss.at[it, j, 0], ring_rs.at[it, j, 0], (sibling, z)
-            )
-            if j == 0:
-                send_masses()
-            k0[j] = jnp.dot(
-                wt[pl.ds(base_half, half), :], xs[:, cols(j)], preferred_element_type=jnp.float32
-            )
-
-        def stage1(j, it=it):
+        def sums1(j, it=it):
             flights[0, j].wait_recv()
-            there, here = pl.ds(theirs_q, quarter), pl.ds(mine_q, quarter)
-            s1[it, j] = (k0[j, there] + r0[it, j, there].astype(jnp.float32)).astype(jnp.bfloat16)
-            flights[1, j] = remote(
-                s1.at[it, j], r1.at[it, j], ring_ss.at[it, j, 1], ring_rs.at[it, j, 1], (first, z)
-            )
-            k1[j] = k0[j, here] + r0[it, j, here].astype(jnp.float32)
-
-        def stage2(j, it=it):
-            flights[1, j].wait_recv()
-            there, here = pl.ds(theirs_e, eighth), pl.ds(mine_e, eighth)
-            s2[it, j] = (k1[j, there] + r1[it, j, there].astype(jnp.float32)).astype(jnp.bfloat16)
-            flights[2, j] = remote(
-                s2.at[it, j], r2.at[it, j], ring_ss.at[it, j, 2], ring_rs.at[it, j, 2], (second, z)
-            )
-            k2[j] = k1[j, here] + r1[it, j, here].astype(jnp.float32)
-            if j == 0:
-                everyone = mass_send[it]
-                for d in range(1, 8):
-                    masses[d - 1].wait_recv()
-                    everyone = everyone + mass_recv[it, d - 1]
-                tall = jnp.concatenate([everyone] * 16, axis=0)
-                mass_col[...] = 1.0 / (jnp.transpose(tall) + PRIOR_WEIGHT)
-
-        def stage3(j, it=it):
-            flights[2, j].wait_recv()
-            mine = pl.ds(base, eighth)
+            both = k0[j] + r0[it, j].astype(jnp.float32)
+            k0[j] = both
+            s1[it, j] = both.astype(jnp.bfloat16)
+            for p in (2, 0, 1):
+                flights[1 + p, j] = remote(
+                    s1.at[it, j, part(chip + flips[p])], r1.at[it, j, p],
+                    ring_ss.at[it, j, 1 + p], ring_rs.at[it, j, 1 + p],
+                    (r + 2 * flips[p], z),
+                )
+
+        def take_masses(it=it):
+            everyone = mass_send[it]
+            for d in range(1, 8):
+                masses[d - 1].wait_recv()
+                everyone = everyone + mass_recv[it, d - 1]
+            tall = jnp.broadcast_to(everyone, (128, count))
+            mass_col[...] = 1.0 / (jnp.transpose(tall) + PRIOR_WEIGHT)
+
+        def update(j, it=it):
+            mine = place(core, chip)
             old = cs[mine, cols(j)] if it == 0 else cc[it - 1, j, mine]
-            sums = k2[j] + r2[it, j].astype(jnp.float32) + PRIOR_WEIGHT * old.astype(jnp.float32)
-            cc[it, j, mine] = (sums * mass_col[mine, 0:1]).astype(jnp.bfloat16)
-            place = cc.at[it, j, mine]
-            flights[3, j] = remote(
-                place, place, ring_ss.at[it, j, 3], ring_rs.at[it, j, 3], (second, z)
-            )
-
-        def stage4(j, it=it):
-            flights[3, j].wait_recv()
-            place = cc.at[it, j, pl.ds(base_quarter, quarter)]
-            flights[4, j] = remote(
-                place, place, ring_ss.at[it, j, 4], ring_rs.at[it, j, 4], (first, z)
-            )
-
-        def stage5(j, it=it):
-            flights[4, j].wait_recv()
-            place = cc.at[it, j, pl.ds(base_half, half)]
-            flights[5, j] = remote(
-                place, place, ring_ss.at[it, j, 5], ring_rs.at[it, j, 5], (sibling, z)
-            )
-
-        def stage6(j, it=it):
-            flights[5, j].wait_recv()
+            blend = k0[j, part(chip)] + PRIOR_WEIGHT * old.astype(jnp.float32)
+            for p in range(3):
+                flights[1 + p, j].wait_recv()
+                blend = blend + r1[it, j, p].astype(jnp.float32)
+            cc[it, j, mine] = (blend * mass_col[mine, 0:1]).astype(jnp.bfloat16)
+            here = cc.at[it, j, mine]
+            for p in (2, 0, 1):
+                flights[4 + p, j] = remote(
+                    here, here, ring_ss.at[it, j, 4 + p], ring_rs.at[it, j, 4 + p],
+                    (r + 2 * flips[p], z),
+                )
+            save(j, 0, mine)
+            flights[7, j] = remote(
+                here, here, ring_ss.at[it, j, 7], ring_rs.at[it, j, 7], (sibling, z)
+            )
+
+        def save(j, n, rows_of, it=it):
             if it == ITERS - 1:
-                copy = pltpu.make_async_copy(cc.at[it, j], out_hbm.at[:, cols(j)], out_sem.at[j])
+                copy = pltpu.make_async_copy(
+                    cc.at[it, j, rows_of], out_hbm.at[rows_of, cols(j)], out_sem.at[j, n]
+                )
                 copy.start()
                 outs.append(copy)
+
+        def forward(j, it=it):
+            for p in range(3):
+                flights[4 + p, j].wait_recv()
+                here = cc.at[it, j, place(core, chip + flips[p])]
+                flights[8 + p, j] = remote(
+                    here, here, ring_ss.at[it, j, 8 + p], ring_rs.at[it, j, 8 + p], (sibling, z)
+                )
+                save(j, 1 + p, place(core, chip + flips[p]))
+
+        def use(j, it=it):
+            for p, flip in enumerate((0,) + flips):
+                flights[7 + p, j].wait_recv()
+                save(j, 4 + p, place(1 - core, chip + flip))
+            if it == ITERS - 1:
                 return
             block = cc[it, j]
             inner = lax.dot_general(block, xs[:, cols(j)], NT, preferred_element_type=jnp.float32)
@@ -261,12 +259,18 @@
                 st[...] += inner
                 sq[...] += norms(block)
 
-        outs = []
-        stages = [stage0, stage1, stage2, stage3, stage4, stage5, stage6]
-        for tick in range(chunks + len(stages) - 1):
-            for s in reversed(range(len(stages))):
-                if 0 <= tick - s < chunks:
-                    stages[s](tick - s)
+        for j in range(chunks):
+            sums0(j)
+        send_masses()
+        for j in range(chunks):
+            sums1(j)
+        take_masses()
+        for j in range(chunks):
+            update(j)
+        for j in range(chunks):
+            forward(j)
+        for j in range(chunks):
+            use(j)
         for copy in outs:
             copy.wait()
 
@@ -279,7 +283,7 @@
     count = centroids.shape[0]
     chunks = CHUNKS
     width = depth // chunks
-    half, quarter, eighth = count // 2, count // 4, count // 8
+    half, share = count // 2, count // 8
     bf16, f32 = jnp.bfloat16, jnp.float32
     dma = pltpu.SemaphoreType.DMA
     result, energy = pl.pallas_call(
@@ -302,29 +306,25 @@
             pltpu.VMEM((count, 128), f32),
             pltpu.VMEM((ITERS, 2, rows), f32),
             pltpu.VMEM((ITERS, groups - 1, 2, rows), f32),
-            pltpu.VMEM((ITERS, 8, count), f32),
-            pltpu.VMEM((ITERS, 7, 8, count), f32),
+            pltpu.VMEM((ITERS, 1, count), f32),
+            pltpu.VMEM((ITERS, 7, 1, count), f32),
             pltpu.VMEM((ITERS, chunks, half, width), bf16),
             pltpu.VMEM((ITERS, chunks, half, width), bf16),
             pltpu.VMEM((chunks, half, width), f32),
-            pltpu.VMEM((ITERS, chunks, quarter, width), bf16),
-            pltpu.VMEM((ITERS, chunks, quarter, width), bf16),
-            pltpu.VMEM((chunks, quarter, width), f32),
-            pltpu.VMEM((ITERS, chunks, eighth, width), bf16),
-            pltpu.VMEM((ITERS, chunks, eighth, width), bf16),
-            pltpu.VMEM((chunks, eighth, width), f32),
+            pltpu.VMEM((ITERS, chunks, half, width), bf16),
+            pltpu.VMEM((ITERS, chunks, 3, share, width), bf16),
             pltpu.VMEM((ITERS, chunks, count, width), bf16),
             dma((2,)),
-            dma((chunks,)),
+            dma((chunks, 8)),
             dma((ITERS, groups - 1)),
             dma((ITERS, groups - 1)),
             dma((ITERS, 7)),
             dma((ITERS, 7)),
-            dma((ITERS, chunks, 6)),
-            dma((ITERS, chunks, 6)),
+            dma((ITERS, chunks, 11)),
+            dma((ITERS, chunks, 11)),
         ],
         compiler_params=pltpu.CompilerParams(
-            collective_id=0, has_side_effects=True, vmem_limit_bytes=48 * 1024 * 1024
+            collective_id=0, has_side_effects=True, vmem_limit_bytes=63 * 1024 * 1024
         ),
         cost_estimate=pl.CostEstimate(
             flops=8 * rows * count * depth,

time: 59.5 us -> 45.9 us (0.77)
  Pallas kernels: 54.7 us -> 42.4 us
  local copies, waits for them, and re-layouts: 3.99 us -> 2.65 us
    pallas_call x1, Pallas kernels: 54.7 us -> 42.4 us  [local_fused(): pl.pallas_call(functools.partial(kernel, groups, chunks), out_shape=(jax....]
    unnamed x6 -> x4, local copies, waits for them, and re-layouts: 3.99 us -> 2.65 us
where the time goes in v2:
time: 45.9 us; the launch traced here: 45.7 us
  Pallas kernels  42.4 us (92%)
  local copies, waits for them, and re-layouts  2.65 us (6%)
  between operations  0.65 us (1%)
    pallas_call x1, Pallas kernels, local_fused(): pl.pallas_call(functools.partial(kernel, groups, chunks), out_shape=(jax....  42.4 us
    unnamed x4, local copies, waits for them, and re-layouts  2.65 us

profile of v2, /device:TPU:1, one launch (start us, length us, event | category | flops | bytes accessed | tf_op | source)
XLA Modules:
  0.0 45.7 jit_solution(17152108428340237742)
XLA Ops:
  0.6 42.4 %shard_map.41 = (bf16[256,1536]{1,0:T(8,128)(2,1)}, f32[1,512]{1,0:T(1,128)}) custom-call(bf16[512,1536]{1,0:T(8,128)(2,1)} %x_hbm.1, bf16[256,1536]{1,0:T(8,128)(2,1)} %c_hbm.1), custom_call_target="tpu_custom_call" | custom-call | flops 1610612736 | bytes 3145728 | tf_op jit(solution)/shard_map/pallas_call | solution.py:289
  43.0 0.0 copy-start
  43.0 2.1 %copy.6 = bf16[256,1536]{1,0:T(8,128)(2,1)} copy(bf16[256,1536]{1,0:T(8,128)(2,1)} %get-tuple-element.8) | data formatting | bytes 1572864
  45.1 0.0 copy-done
  45.1 0.6 %copy.7 = f32[512]{0:T(512)} copy(f32[512]{0:T(512)S(1)} %bitcast.1) | data formatting | bytes 4096
Async XLA Ops:
  43.0 2.1 %copy-start = (f32[1,512]{1,0:T(1,128)S(1)}, f32[1,512]{1,0:T(1,128)}, u32[]{:S(2)}) copy-start(f32[1,512]{1,0:T(1,128)} %get-tuple-element.5) | copy-start | bytes 6148

commit v3 on v2

v3 whole, which is shorter than its diff:
```python
import functools

import jax
import jax.numpy as jnp
from jax import lax
from jax.experimental import pallas as pl
from jax.experimental.pallas import tpu as pltpu
from jax.sharding import PartitionSpec as P

ITERS = 2
PRIOR_WEIGHT = 8.0
CHUNKS = 2
MESH = pl.DeviceIdType.MESH
NT = (((1,), (1,)), ((), ()))


def score_against(embeddings, cluster_block):
    squared = jnp.sum(jnp.square(cluster_block.astype(jnp.float32)), axis=1)
    inner = lax.dot_general(embeddings, cluster_block, NT, preferred_element_type=jnp.float32)
    return inner - 0.5 * squared[None, :]


def updated_rows(totals, mass, previous):
    blended = (totals + PRIOR_WEIGHT * previous.astype(jnp.float32)) / (mass + PRIOR_WEIGHT)[
        :, None
    ]
    return blended.astype(jnp.bfloat16)


def local_plain(embeddings, centroids):
    row_count = embeddings.shape[0]
    cluster_count = centroids.shape[0]
    share_rows = cluster_count // lax.axis_size("row")
    shares = lax.dynamic_slice_in_dim(centroids, lax.axis_index("row") * share_rows, share_rows, 0)
    energy = jnp.zeros((row_count,), jnp.float32)
    for iteration in range(ITERS):
        if iteration == 0:
            scores = score_against(embeddings, centroids)
        else:
            scores = score_against(embeddings, lax.all_gather(shares, "row", axis=0, tiled=True))
        row_top = lax.pmax(jnp.max(scores, axis=1), "cent")
        lifted = jnp.exp(scores - row_top[:, None])
        row_total = lax.psum(jnp.sum(lifted, axis=1), "cent")
        weights = (lifted / row_total[:, None]).astype(jnp.bfloat16)
        totals = lax.dot_general(
            weights, embeddings, (((0,), (0,)), ((), ())), preferred_element_type=jnp.float32
        )
        mass = jnp.sum(weights.astype(jnp.float32), axis=0)
        energies = row_top + jnp.log(row_total)
        if iteration == 0:
            energy = energies
        share_totals, share_mass = (
            lax.psum_scatter(totals, "row", scatter_dimension=0, tiled=True),
            lax.psum_scatter(mass, "row", scatter_dimension=0, tiled=True),
        )
        shares = updated_rows(share_totals, share_mass, shares)
    result = lax.all_gather(shares, "row", axis=0, tiled=True)
    return (result, energy)


def kernel(
    groups, chunks,
    x_hbm, c_hbm, out_hbm, energy_ref,
    xs, cs, wt, st1, er, st2, sq, mass_col,
    stat_send1, stat_recv1, stat_send2, stat_recv2, mass_send, mass_recv,
    k0, s1, r1, cc,
    load_sem, out_sem, x_ss, x_rs, e_ss, e_rs, stat_ss, stat_rs, mass_ss, mass_rs,
    ring_ss, ring_rs,
):
    rows, depth = x_hbm.shape
    count = cs.shape[0]
    width = depth // chunks
    half, share = count // 2, count // 8
    r = lax.axis_index("row")
    z = lax.axis_index("cent")
    core = lax.rem(r, 2)
    px = lax.rem(r // 2, 2)
    py = r // 4
    sibling = r + 1 - 2 * core
    flips = (1 - 2 * px, 2 * (1 - 2 * py), 1 - 2 * px + 2 * (1 - 2 * py))
    chip = r // 2
    my_half = pl.ds(pl.multiple_of(core * half, half), half)
    other_half = pl.ds(pl.multiple_of((1 - core) * half, half), half)
    my_rows = pl.ds(pl.multiple_of(core * rows, rows), rows)
    other_rows = pl.ds(pl.multiple_of((1 - core) * rows, rows), rows)

    def part(owner):
        return pl.ds(pl.multiple_of(owner * share, share), share)

    def place(core_of, owner):
        return pl.ds(pl.multiple_of(core_of * half + owner * share, share), share)

    column = [
        (2 * d + flip - 1, flip, (r + flip * (1 - 2 * core), lax.rem(z + d, groups)))
        for d in range(groups)
        for flip in range(2)
        if d + flip > 0
    ]
    column = sorted(column, key=lambda entry: -entry[0])

    barrier = pltpu.get_barrier_semaphore()
    for _, _, device in column:
        pl.semaphore_signal(barrier, inc=1, device_id=device, device_id_type=MESH)
    for p in range(3):
        pl.semaphore_signal(
            barrier, inc=1, device_id=(r + 2 * flips[p], z), device_id_type=MESH
        )
    loads = [
        pltpu.make_async_copy(x_hbm, xs.at[my_rows], load_sem.at[0]),
        pltpu.make_async_copy(c_hbm, cs, load_sem.at[1]),
    ]
    for load in loads:
        load.start()

    sends = []

    def remote(src, dst, ss, rs, device):
        copy = pltpu.make_async_remote_copy(
            src_ref=src, dst_ref=dst, send_sem=ss, recv_sem=rs,
            device_id=device, device_id_type=MESH,
        )
        copy.start()
        sends.append(copy)
        return copy

    def cols(j):
        return pl.ds(j * width, width)

    def norms(block):
        wide = block.astype(jnp.float32)
        return jnp.sum(wide * wide, axis=1, keepdims=True)

    def soften(scores):
        top = jnp.max(scores, axis=0, keepdims=True)
        lifted = jnp.exp(scores - top)
        return top, lifted, jnp.sum(lifted, axis=0, keepdims=True)

    def combine(found):
        all_top = found[0][0]
        for top, _ in found[1:]:
            all_top = jnp.maximum(all_top, top)
        all_total = found[0][1] * jnp.exp(found[0][0] - all_top)
        for top, total in found[1:]:
            all_total = all_total + total * jnp.exp(top - all_top)
        return all_top, all_total

    def send_stats(it, send, recv):
        return {
            slot: remote(
                send, recv.at[slot], stat_ss.at[it, slot], stat_rs.at[it, slot], device
            )
            for slot, _, device in column
        }

    for load in loads:
        load.wait()
    st1[...] = lax.dot_general(
        cs[...], xs[my_rows, :], NT, preferred_element_type=jnp.float32
    ) - 0.5 * norms(cs[...])
    pl.semaphore_wait(barrier, len(column) + 3)
    top, lifted, total = soften(st1[...])
    stat_send1[0:1, :] = top
    stat_send1[1:2, :] = total
    arrivals = send_stats(0, stat_send1, stat_recv1)
    st1[...] = lifted
    lifted_flight = remote(st1.at[other_half], er, e_ss.at[0], e_rs.at[0], (sibling, z))
    x_flights = [
        remote(
            xs.at[my_rows, cols(j)], xs.at[my_rows, cols(j)],
            x_ss.at[j], x_rs.at[j], (sibling, z),
        )
        for j in range(chunks)
    ]

    for it in range(ITERS):
        if it == 0:
            for slot, _, _ in column:
                arrivals[slot].wait_recv()
            stats = [
                (flip, (stat_recv1[slot, 0:1, :], stat_recv1[slot, 1:2, :]))
                for slot, flip, _ in sorted(column, key=lambda entry: entry[0])
            ]
            own = [(top, total)] + [found for flip, found in stats if flip == 0]
            others = [found for flip, found in stats if flip == 1]
            all_top, all_total = combine(own)
            energy_ref[...] = all_top + jnp.log(all_total)
            scale = jnp.exp(top - all_top) / all_total
            wt[:, my_rows] = (st1[my_half, :] * scale).astype(jnp.bfloat16)
            all_top, all_total = combine(others)
            scale = jnp.exp(others[0][0] - all_top) / all_total
            lifted_flight.wait_recv()
            wt[:, other_rows] = (er[...] * scale).astype(jnp.bfloat16)
        else:
            top, lifted, total = soften(st2[...] - 0.5 * sq[...])
            stat_send2[0:1, :] = top
            stat_send2[1:2, :] = total
            arrivals = send_stats(1, stat_send2, stat_recv2)
            st2[...] = lifted
            for slot, _, _ in column:
                arrivals[slot].wait_recv()
            all_top, all_total = combine(
                [(top, total)]
                + [(stat_recv2[s, 0:1, :], stat_recv2[s, 1:2, :]) for s, _, _ in column]
            )
            scale = jnp.exp(top - all_top) / all_total
            wt[...] = (st2[...] * scale).astype(jnp.bfloat16)

        outs = []
        masses = []
        flights = {}

        def sums(j, it=it):
            if it == 0:
                x_flights[j].wait_recv()
            both = jnp.dot(wt[...], xs[:, cols(j)], preferred_element_type=jnp.float32)
            k0[j] = both
            s1[it, j] = both.astype(jnp.bfloat16)
            for p in (2, 0, 1):
                flights[1 + p, j] = remote(
                    s1.at[it, j, part(chip + flips[p])], r1.at[it, j, p],
                    ring_ss.at[it, j, 1 + p], ring_rs.at[it, j, 1 + p],
                    (r + 2 * flips[p], z),
                )

        def send_masses(it=it):
            mass_send[it] = lax.dot_general(
                jnp.ones((8, 2 * rows), jnp.bfloat16), wt[...], NT,
                preferred_element_type=jnp.float32,
            )[0:1, :]
            for p in range(3):
                masses.append(
                    remote(
                        mass_send.at[it], mass_recv.at[it, p],
                        mass_ss.at[it, p], mass_rs.at[it, p],
                        (r + 2 * flips[p], z),
                    )
                )

        def take_masses(it=it):
            everyone = mass_send[it]
            for p in range(3):
                masses[p].wait_recv()
                everyone = everyone + mass_recv[it, p]
            tall = jnp.broadcast_to(everyone, (128, half))
            mass_col[...] = 1.0 / (jnp.transpose(tall) + PRIOR_WEIGHT)

        def save(j, n, rows_of, it=it):
            copy = pltpu.make_async_copy(
                cc.at[it, j, rows_of], out_hbm.at[rows_of, cols(j)], out_sem.at[j, n]
            )
            copy.start()
            outs.append(copy)

        def share_out(j, n, here, it=it):
            spot = cc.at[it, j, here]
            flights[7 + n, j] = remote(
                spot, spot, ring_ss.at[it, j, 7 + n], ring_rs.at[it, j, 7 + n], (sibling, z)
            )
            save(j, n, here)

        def update(j, it=it):
            mine = place(core, chip)
            old = cs[mine, cols(j)] if it == 0 else cc[it - 1, j, mine]
            blend = k0[j, part(chip)] + PRIOR_WEIGHT * old.astype(jnp.float32)
            for p in range(3):
                flights[1 + p, j].wait_recv()
                blend = blend + r1[it, j, p].astype(jnp.float32)
            cc[it, j, mine] = (blend * mass_col[part(chip), 0:1]).astype(jnp.bfloat16)
            here = cc.at[it, j, mine]
            for p in (2, 0, 1):
                flights[4 + p, j] = remote(
                    here, here, ring_ss.at[it, j, 4 + p], ring_rs.at[it, j, 4 + p],
                    (r + 2 * flips[p], z),
                )
            if it == ITERS - 1:
                share_out(j, 0, mine)

        def gather(j, it=it):
            for p in range(3):
                flights[4 + p, j].wait_recv()
                if it == ITERS - 1:
                    share_out(j, 1 + p, place(core, chip + flips[p]))
            if it < ITERS - 1:
                block = cc[it, j, my_half]
                inner = lax.dot_general(
                    block, xs[:, cols(j)], NT, preferred_element_type=jnp.float32
                )
                if j == 0:
                    st2[...] = inner
                    sq[...] = norms(block)
                else:
                    st2[...] += inner
                    sq[...] += norms(block)

        def finish(j):
            for p, flip in enumerate((0,) + flips):
                flights[7 + p, j].wait_recv()
                save(j, 4 + p, place(1 - core, chip + flip))

        for j in range(chunks):
            sums(j)
            if j == 0:
                send_masses()
        take_masses()
        for j in range(chunks):
            update(j)
        for j in range(chunks):
            gather(j)
        if it == ITERS - 1:
            for j in range(chunks):
                finish(j)
        for copy in outs:
            copy.wait()

    for copy in sends:
        copy.wait_send()


def local_fused(groups, embeddings, centroids):
    rows, depth = embeddings.shape
    count = centroids.shape[0]
    chunks = CHUNKS
    width = depth // chunks
    half, share = count // 2, count // 8
    peers = 2 * groups - 1
    bf16, f32 = jnp.bfloat16, jnp.float32
    dma = pltpu.SemaphoreType.DMA
    result, energy = pl.pallas_call(
        functools.partial(kernel, groups, chunks),
        out_shape=(
            jax.ShapeDtypeStruct((count, depth), bf16),
            jax.ShapeDtypeStruct((1, rows), f32),
        ),
        in_specs=[pl.BlockSpec(memory_space=pl.ANY)] * 2,
        out_specs=(
            pl.BlockSpec(memory_space=pl.ANY),
            pl.BlockSpec(memory_space=pltpu.VMEM),
        ),
        scratch_shapes=[
            pltpu.VMEM((2 * rows, depth), bf16),
            pltpu.VMEM((count, depth), bf16),
            pltpu.VMEM((half, 2 * rows), bf16),
            pltpu.VMEM((count, rows), f32),
            pltpu.VMEM((half, rows), f32),
            pltpu.VMEM((half, 2 * rows), f32),
            pltpu.VMEM((half, 1), f32),
            pltpu.VMEM((half, 128), f32),
            pltpu.VMEM((2, rows), f32),
            pltpu.VMEM((peers, 2, rows), f32),
            pltpu.VMEM((2, 2 * rows), f32),
            pltpu.VMEM((peers, 2, 2 * rows), f32),
            pltpu.VMEM((ITERS, 1, half), f32),
            pltpu.VMEM((ITERS, 3, 1, half), f32),
            pltpu.VMEM((chunks, half, width), f32),
            pltpu.VMEM((ITERS, chunks, half, width), bf16),
            pltpu.VMEM((ITERS, chunks, 3, share, width), bf16),
            pltpu.VMEM((ITERS, chunks, count, width), bf16),
            dma((2,)),
            dma((chunks, 8)),
            dma((chunks,)),
            dma((chunks,)),
            dma((1,)),
            dma((1,)),
            dma((ITERS, peers)),
            dma((ITERS, peers)),
            dma((ITERS, 3)),
            dma((ITERS, 3)),
            dma((ITERS, chunks, 11)),
            dma((ITERS, chunks, 11)),
        ],
        compiler_params=pltpu.CompilerParams(
            collective_id=0, has_side_effects=True, vmem_limit_bytes=63 * 1024 * 1024
        ),
        cost_estimate=pl.CostEstimate(
            flops=8 * rows * count * depth,
            bytes_accessed=2 * depth * (rows + 2 * count),
            transcendentals=2 * rows * count,
        ),
    )(embeddings, centroids)
    return result, energy.reshape(rows)


def solution(mesh):
    def local(embeddings, centroids):
        rows, depth = embeddings.shape
        count = centroids.shape[0]
        groups = mesh.shape["cent"]
        fits = (
            mesh.shape["row"] == 8
            and groups > 1
            and rows % 256 == 0
            and rows <= 1024
            and count == 256
            and depth % (128 * CHUNKS) == 0
        )
        if fits:
            return local_fused(groups, embeddings, centroids)
        return local_plain(embeddings, centroids)

    return jax.shard_map(
        local,
        mesh=mesh,
        in_specs=(P("row", None), P("cent", None)),
        out_specs=(P("cent", None), P("row")),
        check_vma=False,
    )
```

time: 45.9 us -> 43.5 us (0.948)
  Pallas kernels: 42.4 us -> 40 us
    pallas_call x1, Pallas kernels: 42.4 us -> 40 us  [local_fused(): pl.pallas_call(functools.partial(kernel, groups, chunks), out_shape=(jax....]
where the time goes in v3:
time: 43.5 us; the launch traced here: 43.3 us
  Pallas kernels  40 us (92%)
  local copies, waits for them, and re-layouts  2.65 us (6%)
  between operations  0.65 us (1%)
    pallas_call x1, Pallas kernels, local_fused(): pl.pallas_call(functools.partial(kernel, groups, chunks), out_shape=(jax....  40 us
    unnamed x4, local copies, waits for them, and re-layouts  2.65 us

profile of v3, /device:TPU:1, one launch (start us, length us, event | category | flops | bytes accessed | tf_op | source)
XLA Modules:
  0.0 43.3 jit_solution(14078314299570557492)
XLA Ops:
  0.6 40.0 %shard_map.41 = (bf16[256,1536]{1,0:T(8,128)(2,1)}, f32[1,512]{1,0:T(1,128)}) custom-call(bf16[512,1536]{1,0:T(8,128)(2,1)} %x_hbm.1, bf16[256,1536]{1,0:T(8,128)(2,1)} %c_hbm.1), custom_call_target="tpu_custom_call" | custom-call | flops 1610612736 | bytes 3145728 | tf_op jit(solution)/shard_map/pallas_call | solution.py:328
  40.6 0.0 copy-start
  40.7 2.1 %copy.6 = bf16[256,1536]{1,0:T(8,128)(2,1)} copy(bf16[256,1536]{1,0:T(8,128)(2,1)} %get-tuple-element.8) | data formatting | bytes 1572864
  42.7 0.0 copy-done
  42.7 0.6 %copy.7 = f32[512]{0:T(512)} copy(f32[512]{0:T(512)S(1)} %bitcast.1) | data formatting | bytes 4096
Async XLA Ops:
  40.6 2.1 %copy-start = (f32[1,512]{1,0:T(1,128)S(1)}, f32[1,512]{1,0:T(1,128)}, u32[]{:S(2)}) copy-start(f32[1,512]{1,0:T(1,128)} %get-tuple-element.5) | copy-start | bytes 6148

commit v4 on v3

--- a/solution.py
+++ b/solution.py
@@ -9,7 +9,7 @@
 
 ITERS = 2
 PRIOR_WEIGHT = 8.0
-CHUNKS = 2
+CHUNKS = 3
 MESH = pl.DeviceIdType.MESH
 NT = (((1,), (1,)), ((), ()))
 
@@ -328,8 +328,8 @@
     result, energy = pl.pallas_call(
         functools.partial(kernel, groups, chunks),
         out_shape=(
-            jax.ShapeDtypeStruct((count, depth), bf16),
-            jax.ShapeDtypeStruct((1, rows), f32),
+            pltpu.VMEM((count, depth), bf16),
+            pltpu.VMEM((1, rows), f32),
         ),
         in_specs=[pl.BlockSpec(memory_space=pl.ANY)] * 2,
         out_specs=(

time: 43.5 us -> 40.6 us (0.933)
  Pallas kernels: 40 us -> 38.3 us
  local copies, waits for them, and re-layouts: 2.65 us -> 1.46 us
    pallas_call x1, Pallas kernels: 40 us -> 38.3 us  [local_fused(): pl.pallas_call(functools.partial(kernel, groups, chunks), out_shape=(pltp...]
    unnamed x4 -> x2, local copies, waits for them, and re-layouts: 2.65 us -> 1.46 us
where the time goes in v4:
time: 40.6 us; the launch traced here: 40.4 us
  Pallas kernels  38.3 us (94%)
  local copies, waits for them, and re-layouts  1.46 us (4%)
  between operations  0.64 us (2%)
    pallas_call x1, Pallas kernels, local_fused(): pl.pallas_call(functools.partial(kernel, groups, chunks), out_shape=(pltp...  38.3 us
    unnamed x2, local copies, waits for them, and re-layouts  1.46 us

profile of v4, /device:TPU:1, one launch (start us, length us, event | category | flops | bytes accessed | tf_op | source)
XLA Modules:
  0.0 40.4 jit_solution(17090206123058300739)
XLA Ops:
  0.6 38.3 %shard_map.41 = (bf16[256,1536]{1,0:T(8,128)(2,1)S(1)}, f32[1,512]{1,0:T(1,128)S(1)}) custom-call(bf16[512,1536]{1,0:T(8,128)(2,1)} %x_hbm.1, bf16[256,1536]{1,0:T(8,128)(2,1)} %c_hbm.1), custom_call_target="tpu_custom_call" | custom-call | flops 1610612736 | bytes 3145728 | tf_op jit(solution)/shard_map/pallas_call | solution.py:328
  39.0 0.9 %copy.6 = bf16[256,1536]{1,0:T(8,128)(2,1)} copy(bf16[256,1536]{1,0:T(8,128)(2,1)S(1)} %get-tuple-element.6) | data formatting | bytes 1572864
  39.9 0.6 %copy.7 = f32[512]{0:T(512)} copy(f32[512]{0:T(512)S(1)} %bitcast.1) | data formatting | bytes 4096

commit v5 on v4

--- a/solution.py
+++ b/solution.py
@@ -60,11 +60,11 @@
 
 def kernel(
     groups, chunks,
-    x_hbm, c_hbm, out_hbm, energy_ref,
+    x_hbm, c_hbm, out_ref, energy_ref,
     xs, cs, wt, st1, er, st2, sq, mass_col,
     stat_send1, stat_recv1, stat_send2, stat_recv2, mass_send, mass_recv,
     k0, s1, r1, cc,
-    load_sem, out_sem, x_ss, x_rs, e_ss, e_rs, stat_ss, stat_rs, mass_ss, mass_rs,
+    load_sem, x_ss, x_rs, e_ss, e_rs, stat_ss, stat_rs, mass_ss, mass_rs,
     ring_ss, ring_rs,
 ):
     rows, depth = x_hbm.shape
@@ -183,7 +183,7 @@
             own = [(top, total)] + [found for flip, found in stats if flip == 0]
             others = [found for flip, found in stats if flip == 1]
             all_top, all_total = combine(own)
-            energy_ref[...] = all_top + jnp.log(all_total)
+            energy_parts = (all_top, all_total)
             scale = jnp.exp(top - all_top) / all_total
             wt[:, my_rows] = (st1[my_half, :] * scale).astype(jnp.bfloat16)
             all_top, all_total = combine(others)
@@ -205,7 +205,6 @@
             scale = jnp.exp(top - all_top) / all_total
             wt[...] = (st2[...] * scale).astype(jnp.bfloat16)
 
-        outs = []
         masses = []
         flights = {}
 
@@ -244,19 +243,16 @@
             tall = jnp.broadcast_to(everyone, (128, half))
             mass_col[...] = 1.0 / (jnp.transpose(tall) + PRIOR_WEIGHT)
 
-        def save(j, n, rows_of, it=it):
-            copy = pltpu.make_async_copy(
-                cc.at[it, j, rows_of], out_hbm.at[rows_of, cols(j)], out_sem.at[j, n]
+        def spot(j, rows_of, it=it):
+            if it == ITERS - 1:
+                return out_ref.at[rows_of, cols(j)]
+            return cc.at[it, j, rows_of]
+
+        def share_out(j, n, here, it=it):
+            block = spot(j, here)
+            flights[7 + n, j] = remote(
+                block, block, ring_ss.at[it, j, 7 + n], ring_rs.at[it, j, 7 + n], (sibling, z)
             )
-            copy.start()
-            outs.append(copy)
-
-        def share_out(j, n, here, it=it):
-            spot = cc.at[it, j, here]
-            flights[7 + n, j] = remote(
-                spot, spot, ring_ss.at[it, j, 7 + n], ring_rs.at[it, j, 7 + n], (sibling, z)
-            )
-            save(j, n, here)
 
         def update(j, it=it):
             mine = place(core, chip)
@@ -265,8 +261,8 @@
             for p in range(3):
                 flights[1 + p, j].wait_recv()
                 blend = blend + r1[it, j, p].astype(jnp.float32)
-            cc[it, j, mine] = (blend * mass_col[part(chip), 0:1]).astype(jnp.bfloat16)
-            here = cc.at[it, j, mine]
+            here = spot(j, mine)
+            here[...] = (blend * mass_col[part(chip), 0:1]).astype(jnp.bfloat16)
             for p in (2, 0, 1):
                 flights[4 + p, j] = remote(
                     here, here, ring_ss.at[it, j, 4 + p], ring_rs.at[it, j, 4 + p],
@@ -293,14 +289,15 @@
                     sq[...] += norms(block)
 
         def finish(j):
-            for p, flip in enumerate((0,) + flips):
+            for p in range(4):
                 flights[7 + p, j].wait_recv()
-                save(j, 4 + p, place(1 - core, chip + flip))
 
         for j in range(chunks):
             sums(j)
             if j == 0:
                 send_masses()
+        if it == 0:
+            energy_ref[...] = energy_parts[0] + jnp.log(energy_parts[1])
         take_masses()
         for j in range(chunks):
             update(j)
@@ -309,8 +306,6 @@
         if it == ITERS - 1:
             for j in range(chunks):
                 finish(j)
-        for copy in outs:
-            copy.wait()
 
     for copy in sends:
         copy.wait_send()
@@ -333,7 +328,7 @@
         ),
         in_specs=[pl.BlockSpec(memory_space=pl.ANY)] * 2,
         out_specs=(
-            pl.BlockSpec(memory_space=pl.ANY),
+            pl.BlockSpec(memory_space=pltpu.VMEM),
             pl.BlockSpec(memory_space=pltpu.VMEM),
         ),
         scratch_shapes=[
@@ -354,9 +349,8 @@
             pltpu.VMEM((chunks, half, width), f32),
             pltpu.VMEM((ITERS, chunks, half, width), bf16),
             pltpu.VMEM((ITERS, chunks, 3, share, width), bf16),
-            pltpu.VMEM((ITERS, chunks, count, width), bf16),
+            pltpu.VMEM((ITERS - 1, chunks, count, width), bf16),
             dma((2,)),
-            dma((chunks, 8)),
             dma((chunks,)),
             dma((chunks,)),
             dma((1,)),

time: 40.6 us -> 40.3 us (level)
  no operation moved by 1% of the time
where the time goes in v5:
time: 40.3 us; the launch traced here: 40.2 us
  Pallas kernels  38.1 us (95%)
  local copies, waits for them, and re-layouts  1.46 us (4%)
  between operations  0.64 us (2%)
    pallas_call x1, Pallas kernels, local_fused(): pl.pallas_call(functools.partial(kernel, groups, chunks), out_shape=(pltp...  38.1 us
    unnamed x2, local copies, waits for them, and re-layouts  1.46 us

profile of v5, /device:TPU:1, one launch (start us, length us, event | category | flops | bytes accessed | tf_op | source)
XLA Modules:
  0.0 40.2 jit_solution(15723599494217956046)
XLA Ops:
  0.6 38.1 %shard_map.41 = (bf16[256,1536]{1,0:T(8,128)(2,1)S(1)}, f32[1,512]{1,0:T(1,128)S(1)}) custom-call(bf16[512,1536]{1,0:T(8,128)(2,1)} %x_hbm.1, bf16[256,1536]{1,0:T(8,128)(2,1)} %c_hbm.1), custom_call_target="tpu_custom_call" | custom-call | flops 1610612736 | bytes 3145728 | tf_op jit(solution)/shard_map/pallas_call | solution.py:323
  38.7 0.9 %copy.6 = bf16[256,1536]{1,0:T(8,128)(2,1)} copy(bf16[256,1536]{1,0:T(8,128)(2,1)S(1)} %get-tuple-element.6) | data formatting | bytes 1572864
  39.6 0.6 %copy.7 = f32[512]{0:T(512)} copy(f32[512]{0:T(512)S(1)} %bitcast.1) | data formatting | bytes 4096

commit v6 on v5

--- a/solution.py
+++ b/solution.py
@@ -292,10 +292,9 @@
             for p in range(4):
                 flights[7 + p, j].wait_recv()
 
+        send_masses()
         for j in range(chunks):
             sums(j)
-            if j == 0:
-                send_masses()
         if it == 0:
             energy_ref[...] = energy_parts[0] + jnp.log(energy_parts[1])
         take_masses()

time: 40.3 us -> 40.8 us (1.012)
    pallas_call x1, Pallas kernels: 38.1 us -> 38.5 us  [local_fused(): pl.pallas_call(functools.partial(kernel, groups, chunks), out_shape=(pltp...]
where the time goes in v6:
time: 40.8 us; the launch traced here: 40.6 us
  Pallas kernels  38.5 us (94%)
  local copies, waits for them, and re-layouts  1.46 us (4%)
  between operations  0.64 us (2%)
    pallas_call x1, Pallas kernels, local_fused(): pl.pallas_call(functools.partial(kernel, groups, chunks), out_shape=(pltp...  38.5 us
    unnamed x2, local copies, waits for them, and re-layouts  1.46 us

profile of v6, /device:TPU:1, one launch (start us, length us, event | category | flops | bytes accessed | tf_op | source)
XLA Modules:
  0.0 40.6 jit_solution(2620058272515309529)
XLA Ops:
  0.6 38.5 %shard_map.41 = (bf16[256,1536]{1,0:T(8,128)(2,1)S(1)}, f32[1,512]{1,0:T(1,128)S(1)}) custom-call(bf16[512,1536]{1,0:T(8,128)(2,1)} %x_hbm.1, bf16[256,1536]{1,0:T(8,128)(2,1)} %c_hbm.1), custom_call_target="tpu_custom_call" | custom-call | flops 1610612736 | bytes 3145728 | tf_op jit(solution)/shard_map/pallas_call | solution.py:322
  39.2 0.9 %copy.6 = bf16[256,1536]{1,0:T(8,128)(2,1)} copy(bf16[256,1536]{1,0:T(8,128)(2,1)S(1)} %get-tuple-element.6) | data formatting | bytes 1572864
  40.0 0.6 %copy.7 = f32[512]{0:T(512)} copy(f32[512]{0:T(512)S(1)} %bitcast.1) | data formatting | bytes 4096
